TPU v7x, 32 devices: a whole 2x2x4 slice. The times are simulated.
32 devices in a mesh: rep: 8 (over y, x, core), shard: 4 (over z).
Axes of the slice: x: 2, y: 2, z: 4, core: 2. Of those that a mesh axis runs over, the one named last changes fastest.
Arguments:
- grads_matrix: bfloat16 [8, 4, 3, 1024, 1024], P('rep', 'shard'), may hold values from -400 to 400
- grads_vector: bfloat16 [8, 4, 5, 1024], P('rep', 'shard'), may hold values from -6 to 6
- master_matrix: float32 [3, 1024, 1024], P(None, 'shard'), may hold values from -0.1875 to 0.1875
- master_vector: float32 [5, 1024], P(None, 'shard'), may hold values from 0.5 to 1.5
- moment_matrix: float32 [3, 1024, 1024], P(None, 'shard'), may hold values from -4 to 4
- moment_vector: float32 [5, 1024], P(None, 'shard'), may hold values from -4 to 4
- second_matrix: float32 [3, 1024, 1024], P(None, 'shard'), may hold values from 0.05 to 2
- second_vector: float32 [5, 1024], P(None, 'shard'), may hold values from 0.05 to 2
Outputs:
- matrix_master: float32 [3, 1024, 1024], P(None, 'shard')
- vector_master: float32 [5, 1024], P(None, 'shard')
- matrix_moment: float32 [3, 1024, 1024], P(None, 'shard')
- vector_moment: float32 [5, 1024], P(None, 'shard')
- matrix_second: float32 [3, 1024, 1024], P(None, 'shard')
- vector_second: float32 [5, 1024], P(None, 'shard')
- matrix_weights: bfloat16 [3, 1024, 1024], replicated
- vector_weights: bfloat16 [5, 1024], replicated
All inputs are finite; a program needn't handle non-finite values.
Results may differ from a plain program's by a relative error of at most 0.005.
Values may be sent and summed in bfloat16 or wider, within the bound.
A program may use at most 128 MiB of HBM per device.

v0:
```python
import jax
import jax.numpy as jnp
from jax import lax
from jax.sharding import PartitionSpec as P

STEP = 1000
beta_first = 0.9
beta_second = 0.999
learn_rate = 0.01
decay_rate = 0.1
epsilon = 1e-08


def adam_piece(total, master, moment, second, clip, decay):
    scaled = total * clip
    moment_next = beta_first * moment + (1.0 - beta_first) * scaled
    second_next = beta_second * second + (1.0 - beta_second) * scaled * scaled
    corrected = moment_next / (1.0 - beta_first**STEP)
    spread = jnp.sqrt(second_next / (1.0 - beta_second**STEP))
    update = corrected / (spread + epsilon)
    master_next = master - learn_rate * (update + decay * master)
    return (master_next, moment_next, second_next)


def squares_of(first, second):
    return jnp.sum(first * first) + jnp.sum(second * second)


def body(
    grads_matrix,
    grads_vector,
    master_matrix,
    master_vector,
    moment_matrix,
    moment_vector,
    second_matrix,
    second_vector,
):
    local_matrix = grads_matrix[0, 0].astype(jnp.float32)
    local_vector = grads_vector[0, 0].astype(jnp.float32)
    width = local_vector.shape[1]
    count = 3 * width * width + 5 * width
    part_matrix, part_vector = (
        lax.psum_scatter(
            local_matrix.astype(jnp.bfloat16), "shard", scatter_dimension=1, tiled=True
        ).astype(jnp.float32),
        lax.psum_scatter(
            local_vector.astype(jnp.bfloat16), "shard", scatter_dimension=1, tiled=True
        ).astype(jnp.float32),
    )
    mine_matrix, mine_vector = (
        lax.psum(part_matrix.astype(jnp.bfloat16), "rep").astype(jnp.float32),
        lax.psum(part_vector.astype(jnp.bfloat16), "rep").astype(jnp.float32),
    )
    squares = lax.psum(squares_of(mine_matrix, mine_vector), "shard")
    clip = jnp.minimum(1.0, 1.0 / jnp.sqrt(squares / count + 1e-06))
    master_mat, moment_mat, second_mat = adam_piece(
        mine_matrix, master_matrix, moment_matrix, second_matrix, clip, decay_rate
    )
    master_vec, moment_vec, second_vec = adam_piece(
        mine_vector, master_vector, moment_vector, second_vector, clip, 0.0
    )
    weights_mat, weights_vec = (
        lax.all_gather(master_mat.astype(jnp.bfloat16), "shard", axis=1, tiled=True),
        lax.all_gather(master_vec.astype(jnp.bfloat16), "shard", axis=1, tiled=True),
    )
    return (
        master_mat,
        master_vec,
        moment_mat,
        moment_vec,
        second_mat,
        second_vec,
        weights_mat,
        weights_vec,
    )


def solution(mesh):
    return jax.shard_map(
        body,
        mesh=mesh,
        in_specs=(
            P("rep", "shard", None, None, None),
            P("rep", "shard", None, None),
            P(None, "shard", None),
            P(None, "shard"),
            P(None, "shard", None),
            P(None, "shard"),
            P(None, "shard", None),
            P(None, "shard"),
        ),
        out_specs=(
            P(None, "shard", None),
            P(None, "shard"),
            P(None, "shard", None),
            P(None, "shard"),
            P(None, "shard", None),
            P(None, "shard"),
            P(),
            P(),
        ),
        check_vma=False,
    )
```

profile of v0, /device:TPU:0, one launch (start us, length us, event | category | flops | bytes accessed | tf_op | source)
XLA Modules:
  0.0 356.3 jit_solution(2101009983233991101)
XLA Ops:
  7.2 0.0 reduce-scatter.3.cloned.1.call-start
  7.2 0.7 reduce-scatter.3.cloned.1.call-update
  7.9 0.0 copy-start
  7.9 0.0 reduce-scatter.5.cloned.1.call-start
  8.0 0.7 reduce-scatter.5.cloned.1.call-update
  8.7 0.0 all-reduce.2.cloned.1.call-start
  8.7 115.1 %reduce-scatter.3.cloned.1.call-done = bf16[3,256,1024]{2,1,0:T(8,128)(2,1)} async-done(((bf16[3,1024,1024]{2,1,0:T(8,128)(2,1)}), bf16[3,256,1024]{2,1,0:T(8,128)(2,1)}) %reduce-scatter.3.cloned.1.call-update) | async-done | bytes 1572880 | tf_op jit(solution)/shard_map/reduce_scatter | solution.py:44
  123.8 0.0 all-reduce.2.cloned.1.call-update
  123.8 0.0 all-gather.2.cloned.1.call-start
  123.9 21.6 %reduce-scatter.5.cloned.1.call-done = bf16[5,256]{1,0:T(8,128)(2,1)} async-done(((bf16[5,1024]{1,0:T(8,128)(2,1)}), bf16[5,256]{1,0:T(8,128)(2,1)}) %reduce-scatter.5.cloned.1.call-update) | async-done | bytes 2576 | tf_op jit(solution)/shard_map/reduce_scatter | solution.py:47
  145.4 12.0 %psum.22 = bf16[5,256]{1,0:T(8,128)(2,1)S(1)} all-reduce(bf16[5,256]{1,0:T(8,128)(2,1)} %reduce-scatter.5.cloned.1.call-done), channel_id=1, replica_groups=mesh['rep'=8,'shard'=4] {'rep'}, use_global_device_ids=true, to_apply=%region_4.0 | all-reduce | flops 1280 | bytes 5120 | tf_op jit(solution)/shard_map/psum | solution.py:53
  157.5 0.6 fusion.6
  158.1 48.1 %all-reduce.2.cloned.1.call-done = bf16[3,256,1024]{2,1,0:T(8,128)(2,1)} async-done(((bf16[3,256,1024]{2,1,0:T(8,128)(2,1)}), bf16[3,256,1024]{2,1,0:T(8,128)(2,1)}) %all-reduce.2.cloned.1.call-update) | async-done | bytes 1572880 | tf_op jit(solution)/shard_map/psum | solution.py:52
  206.2 2.8 fusion.2
  210.3 12.3 %psum.23 = f32[]{:T(128)} all-reduce(f32[]{:T(128)S(6)} %add.46), channel_id=1, replica_groups=mesh['rep'=8,'shard'=4] {'shard'}, use_global_device_ids=true, to_apply=%region_6.0 | all-reduce | flops 1 | bytes 8 | tf_op jit(solution)/shard_map/psum | solution.py:55
  223.3 0.0 copy-done
  223.4 0.0 copy-start.1
  223.4 0.0 copy-start.2
  223.4 0.0 copy-start.3
  223.4 7.5 %fusion.11 = (bf16[3,256,1024]{2,1,0:T(8,128)(2,1)}, f32[3,256,1024]{2,1,0:T(8,128)}, f32[3,256,1024]{2,1,0:T(8,128)}, f32[3,256,1024]{2,1,0:T(8,128)}) fusion(f32[3,256,1024]{2,1,0:T(8,128)S(1)} %copy-done, f32[]{:T(128)S(6)} %min.3, bf16[3,256,1024]{2,1,0:T(8,128)(2,1)} %all-reduce.2.cloned.1.call-done, f32[3,256,1024]{2,1,0:T(8,128)} %param.14, ...), kind=kLoop, calls=%fused_computation.17 | loop fusion | flops 13369344 | bytes 22020100 | tf_op jit(solution)/shard_map/convert_element_type | solution.py:64
  230.9 0.0 all-gather.2.cloned.1.call-update
  230.9 0.0 copy-done.1
  230.9 0.0 copy-done.2
  230.9 0.0 copy-done.3
  231.0 0.6 fusion.8
  231.6 13.2 %all_gather.7 = bf16[5,1024]{1,0:T(8,128)(2,1)S(1)} all-gather(bf16[5,256]{1,0:T(8,128)(2,1)S(1)} %get-tuple-element.8), channel_id=1, replica_groups=mesh['rep'=8,'shard'=4] {'shard'}, dimensions={1}, use_global_device_ids=true | all-gather | bytes 12800 | tf_op jit(solution)/shard_map/all_gather | solution.py:65
  244.8 98.1 %all-gather.2.cloned.1.call-done = bf16[3,1024,1024]{2,1,0:T(8,128)(2,1)} async-done(((bf16[3,256,1024]{2,1,0:T(8,128)(2,1)}), bf16[3,1024,1024]{2,1,0:T(8,128)(2,1)}) %all-gather.2.cloned.1.call-update) | async-done | bytes 6291472 | tf_op jit(solution)/shard_map/all_gather | solution.py:64
  342.9 6.2 %copy.19 = bf16[3,1024,1024]{2,1,0:T(8,128)(2,1)} copy(bf16[3,1024,1024]{2,1,0:T(8,128)(2,1)} %all-gather.2.cloned.1.call-done) | data formatting | bytes 12582912
  349.1 0.6 copy.20
Async XLA Ops:
  7.2 116.6 %reduce-scatter.3.cloned.1.call-start = ((), (), s32[]{:S(2)}) async-start(), calls=%async_computation.2 | async-start | bytes 7864320 | tf_op jit(solution)/shard_map/reduce_scatter | solution.py:44
  7.9 215.5 %copy-start = (f32[3,256,1024]{2,1,0:T(8,128)S(1)}, f32[3,256,1024]{2,1,0:T(8,128)}, u32[]{:S(2)}) copy-start(f32[3,256,1024]{2,1,0:T(8,128)} %param.10) | copy-start | bytes 9437188
  7.9 137.5 %reduce-scatter.5.cloned.1.call-start = ((), (), s32[]{:S(2)}) async-start(), calls=%async_computation.4 | async-start | bytes 20480 | tf_op jit(solution)/shard_map/reduce_scatter | solution.py:47
  8.7 197.5 %all-reduce.2.cloned.1.call-start = ((), (), s32[]{:S(2)}) async-start(), calls=%async_computation.3 | async-start | bytes 3145728 | tf_op jit(solution)/shard_map/psum | solution.py:52
  123.8 219.1 %all-gather.2.cloned.1.call-start = ((), (), s32[]{:S(2)}) async-start(), calls=%async_computation.5 | async-start | bytes 7864320 | tf_op jit(solution)/shard_map/all_gather | solution.py:64
  223.4 7.6 %copy-start.1 = (f32[5,256]{1,0:T(8,128)S(1)}, f32[5,256]{1,0:T(8,128)}, u32[]{:S(2)}) copy-start(f32[5,256]{1,0:T(8,128)} %param.11) | copy-start | bytes 15364
  223.4 7.6 %copy-start.2 = (f32[5,256]{1,0:T(8,128)S(1)}, f32[5,256]{1,0:T(8,128)}, u32[]{:S(2)}) copy-start(f32[5,256]{1,0:T(8,128)} %param.15) | copy-start | bytes 15364
  223.4 7.6 %copy-start.3 = (f32[5,256]{1,0:T(8,128)S(1)}, f32[5,256]{1,0:T(8,128)}, u32[]{:S(2)}) copy-start(f32[5,256]{1,0:T(8,128)} %param.13) | copy-start | bytes 15364
Sparse Core Ops, SparseCore 0:
  10.3 113.4 reduce-scatter.2
  126.0 19.3 reduce-scatter.4
  149.0 57.1 all-reduce.1
  231.0 111.8 all-gather.1
where the time goes:
time: 357 us; the launch traced here: 356 us
  waiting for transfers between devices  284 us (80%)
  blocking collectives  37.6 us (11%)
  between operations  15.8 us (4%)
  other arithmetic  11.6 us (3%)
  local copies, waits for them, and re-layouts  6.82 us (2%)
    reduce_scatter x1, waiting for transfers between devices, body(): lax.psum_scatter(local_matrix.astype(jnp.bfloat16), 'shard', scatter_dime...  115 us
    all_gather x1, waiting for transfers between devices, body(): lax.all_gather(master_mat.astype(jnp.bfloat16), 'shard', axis=1, tiled=True)  98.1 us
    psum x1, waiting for transfers between devices, body(): lax.psum(part_matrix.astype(jnp.bfloat16), 'rep').astype(jnp.float32)  48.1 us
    reduce_scatter x1, waiting for transfers between devices, body(): lax.psum_scatter(local_vector.astype(jnp.bfloat16), 'shard', scatter_dime...  21.6 us
    all_gather x1, blocking collectives, body(): lax.all_gather(master_vec.astype(jnp.bfloat16), 'shard', axis=1, tiled=True)  13.2 us
    psum x1, blocking collectives, body(): squares = lax.psum(squares_of(mine_matrix, mine_vector), 'shard')  12.3 us
    psum x1, blocking collectives, body(): lax.psum(part_vector.astype(jnp.bfloat16), 'rep').astype(jnp.float32)  12 us
    convert_element_type x1, other arithmetic, body(): master_mat.astype(jnp.bfloat16)  7.51 us
  transfers between devices with their start and end apart: 4, of which 4 were waited for; matrix products, arithmetic and copies ran while one was open for 0% of the time, Pallas kernels for 0%

commit v1 on v0

--- a/solution.py
+++ b/solution.py
@@ -9,6 +9,27 @@
 learn_rate = 0.01
 decay_rate = 0.1
 epsilon = 1e-08
+
+
+def ring_gather(x, axis, dim):
+    size, index, rows = (lax.axis_size(axis), lax.axis_index(axis), x.shape[dim])
+    right = [(i, (i + 1) % size) for i in range(size)]
+    left = [(i, (i - 1) % size) for i in range(size)]
+    whole = jnp.zeros((*x.shape[:dim], size * rows, *x.shape[dim + 1 :]), x.dtype)
+    whole = lax.dynamic_update_slice_in_dim(whole, x, index * rows, axis=dim)
+    from_left = from_right = x
+    middle = size // 2
+    for step in range(1, middle + 1):
+        from_left = lax.ppermute(from_left, axis, right)
+        whole = lax.dynamic_update_slice_in_dim(
+            whole, from_left, (index - step) % size * rows, axis=dim
+        )
+        if step < size - middle:
+            from_right = lax.ppermute(from_right, axis, left)
+            whole = lax.dynamic_update_slice_in_dim(
+                whole, from_right, (index + step) % size * rows, axis=dim
+            )
+    return whole
 
 
 def adam_piece(total, master, moment, second, clip, decay):
@@ -61,7 +82,7 @@
         mine_vector, master_vector, moment_vector, second_vector, clip, 0.0
     )
     weights_mat, weights_vec = (
-        lax.all_gather(master_mat.astype(jnp.bfloat16), "shard", axis=1, tiled=True),
+        ring_gather(master_mat.astype(jnp.bfloat16), "shard", 1),
         lax.all_gather(master_vec.astype(jnp.bfloat16), "shard", axis=1, tiled=True),
     )
     return (

time: 357 us -> 357 us (level)
  waiting for transfers between devices: 284 us -> 222 us
  blocking collectives: 37.6 us -> 94.1 us
  starting transfers between devices: 0.15 us -> 3.94 us
    all_gather x1 -> x0, waiting for transfers between devices: 98.1 us -> none  [body(): lax.all_gather(master_mat.astype(jnp.bfloat16), 'shard', axis=1, tiled=True)]
    all_gather x1, blocking collectives: 13.2 us -> 69.7 us  [body(): lax.all_gather(master_vec.astype(jnp.bfloat16), 'shard', axis=1, tiled=True)]
    ppermute x0 -> x3, waiting for transfers between devices: none -> 35.5 us  [the longest x2 35.5 us: ring_gather(): from_left = lax.ppermute(from_left, axis, right)]
    convert_element_type x1 -> x0, other arithmetic: 7.51 us -> none  [body(): master_mat.astype(jnp.bfloat16)]
    dynamic_update_slice x0 -> x1, other arithmetic: none -> 7.3 us  [ring_gather(): whole = lax.dynamic_update_slice_in_dim(whole, x, index * rows, axis=dim)]
    unnamed x10 -> x13, local copies, waits for them, and re-layouts: 6.82 us -> 0.81 us
    dynamic_update_slice x0 -> x3, local copies, waits for them, and re-layouts: none -> 5.19 us  [the longest x1 2.67 us: ring_gather(): lax.dynamic_update_slice_in_dim(whole, from_right, (index + step) % size...]
    ppermute x0 -> x3, starting transfers between devices: none -> 3.83 us  [the longest x1 3.82 us: ring_gather(): from_right = lax.ppermute(from_right, axis, left)]
  transfers between devices with their start and end apart: 4 -> 6, of which waited for: 4 -> 4; matrix products, arithmetic and copies ran while one was open for 0% -> 1% of each run, Pallas kernels for 0% -> 0%
where the time goes in v1:
time: 357 us
  waiting for transfers between devices  222 us (62%)
  blocking collectives  94.1 us (26%)
  between operations  15.8 us (4%)
  other arithmetic  11.5 us (3%)
  local copies, waits for them, and re-layouts  9.6 us (3%)
  starting transfers between devices  3.94 us (1%)
    reduce_scatter x1, waiting for transfers between devices, body(): lax.psum_scatter(local_matrix.astype(jnp.bfloat16), 'shard', scatter_dime...  115 us
    all_gather x1, blocking collectives, body(): lax.all_gather(master_vec.astype(jnp.bfloat16), 'shard', axis=1, tiled=True)  69.7 us
    psum x1, waiting for transfers between devices, body(): lax.psum(part_matrix.astype(jnp.bfloat16), 'rep').astype(jnp.float32)  48.1 us
    ppermute x2, waiting for transfers between devices, ring_gather(): from_left = lax.ppermute(from_left, axis, right)  35.5 us
    reduce_scatter x1, waiting for transfers between devices, body(): lax.psum_scatter(local_vector.astype(jnp.bfloat16), 'shard', scatter_dime...  21.6 us
    psum x1, blocking collectives, body(): squares = lax.psum(squares_of(mine_matrix, mine_vector), 'shard')  12.3 us
    psum x1, blocking collectives, body(): lax.psum(part_vector.astype(jnp.bfloat16), 'rep').astype(jnp.float32)  12 us
    dynamic_update_slice x1, other arithmetic, ring_gather(): whole = lax.dynamic_update_slice_in_dim(whole, x, index * rows, axis=dim)  7.3 us
  transfers between devices with their start and end apart: 6, of which 4 were waited for; matrix products, arithmetic and copies ran while one was open for 1% of the time, Pallas kernels for 0%

profile of v1, /device:TPU:0, one launch (start us, length us, event | category | flops | bytes accessed | tf_op | source)
XLA Modules:
  0.0 356.7 jit_solution(16911491516338478768)
XLA Ops:
  7.2 0.0 reduce-scatter.3.cloned.1.call-start
  7.2 0.7 reduce-scatter.3.cloned.1.call-update
  7.9 0.0 reduce-scatter.5.cloned.1.call-start
  7.9 0.7 reduce-scatter.5.cloned.1.call-update
  8.6 0.0 all-reduce.2.cloned.1.call-start
  8.7 115.1 %reduce-scatter.3.cloned.1.call-done = bf16[3,256,1024]{2,1,0:T(8,128)(2,1)} async-done(((bf16[3,1024,1024]{2,1,0:T(8,128)(2,1)}), bf16[3,256,1024]{2,1,0:T(8,128)(2,1)}) %reduce-scatter.3.cloned.1.call-update) | async-done | bytes 1572880 | tf_op jit(solution)/shard_map/reduce_scatter | solution.py:65
  123.8 0.0 all-reduce.2.cloned.1.call-update
  123.8 21.6 %reduce-scatter.5.cloned.1.call-done = bf16[5,256]{1,0:T(8,128)(2,1)} async-done(((bf16[5,1024]{1,0:T(8,128)(2,1)}), bf16[5,256]{1,0:T(8,128)(2,1)}) %reduce-scatter.5.cloned.1.call-update) | async-done | bytes 2576 | tf_op jit(solution)/shard_map/reduce_scatter | solution.py:68
  145.4 12.0 %psum.22 = bf16[5,256]{1,0:T(8,128)(2,1)S(1)} all-reduce(bf16[5,256]{1,0:T(8,128)(2,1)} %reduce-scatter.5.cloned.1.call-done), channel_id=1, replica_groups=mesh['rep'=8,'shard'=4] {'rep'}, use_global_device_ids=true, to_apply=%region_4.0 | all-reduce | flops 1280 | bytes 5120 | tf_op jit(solution)/shard_map/psum | solution.py:74
  157.5 0.6 fusion.6
  158.1 48.1 %all-reduce.2.cloned.1.call-done = bf16[3,256,1024]{2,1,0:T(8,128)(2,1)} async-done(((bf16[3,256,1024]{2,1,0:T(8,128)(2,1)}), bf16[3,256,1024]{2,1,0:T(8,128)(2,1)}) %all-reduce.2.cloned.1.call-update) | async-done | bytes 1572880 | tf_op jit(solution)/shard_map/psum | solution.py:73
  206.2 0.0 copy-start.2
  206.2 3.0 fusion.2
  210.5 12.3 %psum.23 = f32[]{:T(128)} all-reduce(f32[]{:T(128)S(6)} %add.73), channel_id=1, replica_groups=mesh['rep'=8,'shard'=4] {'shard'}, use_global_device_ids=true, to_apply=%region_6.0 | all-reduce | flops 1 | bytes 8 | tf_op jit(solution)/shard_map/psum | solution.py:76
  223.5 0.0 copy-start
  223.5 0.0 copy-start.1
  223.5 3.6 %broadcast_in_dim.3 = bf16[3,1024,1024]{2,1,0:T(8,128)(2,1)} broadcast(bf16[]{:T(256)} %constant.64.clone.1), dimensions={} | broadcast | bytes 6291458 | tf_op jit(solution)/shard_map/broadcast_in_dim | solution.py:18
  227.1 0.0 copy-done.2
  227.1 0.0 copy-done
  227.1 0.2 copy-done.1
  227.3 0.0 copy-start.3
  227.3 0.0 copy-start.4
  227.3 0.0 copy-start.5
  227.3 7.3 %constant_dynamic-update-slice_fusion.3 = (bf16[3,1024,1024]{2,1,0:T(8,128)(2,1)}, bf16[3,256,1024]{2,1,0:T(8,128)(2,1)}, f32[3,256,1024]{2,1,0:T(8,128)}, f32[3,256,1024]{2,1,0:T(8,128)}, f32[3,256,1024]{2,1,0:T(8,128)}) fusion(bf16[3,1024,1024]{2,1,0:T(8,128)(2,1)} %broadcast_in_dim.3, s32[]{:T(128)S(6)} %select_n.27, f32[3,256,1024]{2,1,0:T(8,128)S(1)} %copy-done.1, ...), kind=kLoop, calls=%fused_computation.19 | loop fusion | flops 13369344 | bytes 23592968 | tf_op jit(solution)/shard_map/dynamic_update_slice | solution.py:19
  234.6 0.0 collective-permute-start
  234.6 3.8 %collective-permute-start.1 = (bf16[3,256,1024]{2,1,0:T(8,128)(2,1)}, bf16[3,256,1024]{2,1,0:T(8,128)(2,1)}, u32[]{:S(2)}, u32[]{:S(2)}) collective-permute-start(bf16[3,256,1024]{2,1,0:T(8,128)(2,1)} %get-tuple-element.13), channel_id=1, source_target_pairs={{0,3},{1,0},{2,1},{3,2},{4,7},{5,4},{6,5},{7,6},{8,11},{9,8},{10,9... | collective-permute-start | bytes 4718600 | tf_op jit(solution)/shard_map/ppermute | solution.py:28
  238.4 35.5 %collective-permute-done = bf16[3,256,1024]{2,1,0:T(8,128)(2,1)S(1)} collective-permute-done((bf16[3,256,1024]{2,1,0:T(8,128)(2,1)}, bf16[3,256,1024]{2,1,0:T(8,128)(2,1)S(1)}, u32[]{:S(2)}, u32[]{:S(2)}) %collective-permute-start) | collective-permute-done | bytes 1572896 | tf_op jit(solution)/shard_map/ppermute | solution.py:23
  274.0 0.0 collective-permute-start.2
  274.0 0.0 copy-done.3
  274.0 0.0 copy-done.4
  274.0 0.0 copy-done.5
  274.0 0.6 fusion.8
  274.6 69.7 %all_gather.3 = bf16[5,1024]{1,0:T(8,128)(2,1)S(1)} all-gather(bf16[5,256]{1,0:T(8,128)(2,1)S(1)} %get-tuple-element.8), channel_id=1, replica_groups=mesh['rep'=8,'shard'=4] {'shard'}, dimensions={1}, use_global_device_ids=true | all-gather | bytes 12800 | tf_op jit(solution)/shard_map/all_gather | solution.py:86
  344.3 1.3 constant_dynamic-update-slice_fusion.2
  345.6 0.0 collective-permute-done.1
  345.6 2.7 constant_dynamic-update-slice_fusion.1
  348.3 0.0 collective-permute-done.2
  348.3 1.3 constant_dynamic-update-slice_fusion
  349.5 0.6 copy.22
Async XLA Ops:
  7.2 116.6 %reduce-scatter.3.cloned.1.call-start = ((), (), s32[]{:S(2)}) async-start(), calls=%async_computation.2 | async-start | bytes 7864320 | tf_op jit(solution)/shard_map/reduce_scatter | solution.py:65
  7.9 137.5 %reduce-scatter.5.cloned.1.call-start = ((), (), s32[]{:S(2)}) async-start(), calls=%async_computation.4 | async-start | bytes 20480 | tf_op jit(solution)/shard_map/reduce_scatter | solution.py:68
  8.6 197.5 %all-reduce.2.cloned.1.call-start = ((), (), s32[]{:S(2)}) async-start(), calls=%async_computation.3 | async-start | bytes 3145728 | tf_op jit(solution)/shard_map/psum | solution.py:73
  206.2 20.9 %copy-start.2 = (f32[3,256,1024]{2,1,0:T(8,128)S(1)}, f32[3,256,1024]{2,1,0:T(8,128)}, u32[]{:S(2)}) copy-start(f32[3,256,1024]{2,1,0:T(8,128)} %param.14) | copy-start | bytes 9437188
  223.5 3.6 %copy-start = (bf16[3,256,1024]{2,1,0:T(8,128)(2,1)S(1)}, bf16[3,256,1024]{2,1,0:T(8,128)(2,1)}, u32[]{:S(2)}) copy-start(bf16[3,256,1024]{2,1,0:T(8,128)(2,1)} %all-reduce.2.cloned.1.call-done) | copy-start | bytes 4718596
  223.5 3.8 %copy-start.1 = (f32[3,256,1024]{2,1,0:T(8,128)S(1)}, f32[3,256,1024]{2,1,0:T(8,128)}, u32[]{:S(2)}) copy-start(f32[3,256,1024]{2,1,0:T(8,128)} %param.10) | copy-start | bytes 9437188
  227.3 46.7 %copy-start.3 = (f32[5,256]{1,0:T(8,128)S(1)}, f32[5,256]{1,0:T(8,128)}, u32[]{:S(2)}) copy-start(f32[5,256]{1,0:T(8,128)} %param.11) | copy-start | bytes 15364
  227.3 46.7 %copy-start.4 = (f32[5,256]{1,0:T(8,128)S(1)}, f32[5,256]{1,0:T(8,128)}, u32[]{:S(2)}) copy-start(f32[5,256]{1,0:T(8,128)} %param.15) | copy-start | bytes 15364
  227.3 46.7 %copy-start.5 = (f32[5,256]{1,0:T(8,128)S(1)}, f32[5,256]{1,0:T(8,128)}, u32[]{:S(2)}) copy-start(f32[5,256]{1,0:T(8,128)} %param.13) | copy-start | bytes 15364
  234.6 39.3 %collective-permute-start = (bf16[3,256,1024]{2,1,0:T(8,128)(2,1)}, bf16[3,256,1024]{2,1,0:T(8,128)(2,1)S(1)}, u32[]{:S(2)}, u32[]{:S(2)}) collective-permute-start(bf16[3,256,1024]{2,1,0:T(8,128)(2,1)} %get-tuple-element.13), channel_id=1, source_target_pairs={{0,1},{1,2},{2,3},{3,0},{4,5},{5,6},{6,7},{7,4},{8,9},{9,10},{10,1... | collective-permute-start | bytes 4718600 | tf_op jit(solution)/shard_map/ppermute | solution.py:23
  234.6 111.0 %collective-permute-start.1 = (bf16[3,256,1024]{2,1,0:T(8,128)(2,1)}, bf16[3,256,1024]{2,1,0:T(8,128)(2,1)}, u32[]{:S(2)}, u32[]{:S(2)}) collective-permute-start(bf16[3,256,1024]{2,1,0:T(8,128)(2,1)} %get-tuple-element.13), channel_id=1, source_target_pairs={{0,3},{1,0},{2,1},{3,2},{4,7},{5,4},{6,5},{7,6},{8,11},{9,8},{10,9... | collective-permute-start | bytes 4718600 | tf_op jit(solution)/shard_map/ppermute | solution.py:28
  274.0 74.3 %collective-permute-start.2 = (bf16[3,256,1024]{2,1,0:T(8,128)(2,1)S(1)}, bf16[3,256,1024]{2,1,0:T(8,128)(2,1)S(1)}, u32[]{:S(2)}, u32[]{:S(2)}) collective-permute-start(bf16[3,256,1024]{2,1,0:T(8,128)(2,1)S(1)} %collective-permute-done), channel_id=1, source_target_pairs={{0,1},{1,2},{2,3},{3,0},{4,5},{5,6},{6,7},{7,4},{8,9},{9,10},{10,1... | collective-permute-start | bytes 4718600 | tf_op jit(solution)/shard_map/ppermute | solution.py:23
Sparse Core Ops, SparseCore 0:
  10.3 113.4 reduce-scatter.2
  126.0 19.3 reduce-scatter.4
  149.0 57.1 all-reduce.1
